TPU v7x, 32 devices: a whole 2x2x4 slice. The times are simulated.
32 devices in a mesh: section: 4 (over y, x), dp: 8 (over z, core).
Axes of the slice: x: 2, y: 2, z: 4, core: 2. Of those that a mesh axis runs over, the one named last changes fastest.
Arguments:
- acts: bfloat16 [4, 9, 32, 32, 128], P('section', None, 'dp'), may hold values from -6 to 6
- kernels: bfloat16 [4, 3, 3, 3, 128, 128], P('section'), may hold values from -0.078125 to 0.078125
- cotangent: bfloat16 [9, 32, 32, 128], P(None, 'dp'), may hold values from -6 to 6
Outputs:
- input_grads: bfloat16 [4, 9, 32, 32, 128], P('section', None, 'dp')
- kernel_grads: float32 [4, 128, 27, 128], P('section', 'dp')
All inputs are finite; a program needn't handle non-finite values.
Results may differ from a plain program's by a relative error of at most 0.03.
Values may be sent and summed in bfloat16 or wider, within the bound.
A program may use at most 128 MiB of HBM per device.

v0:
```python
import math

import jax
import jax.numpy as jnp
from jax import lax
from jax.sharding import PartitionSpec as P


def padded_2(block, sides, width):
    for axis, dim in sides:
        count = lax.axis_size(axis)
        forward = [(i, i + 1) for i in range(count - 1)]
        backward = [(target, source) for source, target in forward]
        low = lax.ppermute(
            lax.slice_in_dim(block, block.shape[dim] - width, None, axis=dim), axis, forward
        )
        high = lax.ppermute(lax.slice_in_dim(block, 0, width, axis=dim), axis, backward)
        block = jnp.concatenate([low, block, high], axis=dim)
    return block


def shifted(block, axis, distance):
    devices = range(lax.axis_size(axis))
    route = [(i - distance, i) for i in devices if i - distance in devices]
    return lax.ppermute(block, axis, route)


def grad_update(padded, kern, grad, slope, col_pad):
    flipped = jnp.swapaxes(kern[::-1, ::-1, ::-1], 3, 4)
    back = lax.conv_general_dilated(
        padded[None],
        flipped,
        (1, 1, 1),
        ((0, 2), (0, 0), (col_pad, col_pad)),
        dimension_numbers=("NDHWC", "DHWIO", "NDHWC"),
        preferred_element_type=jnp.float32,
    )[0]
    return (grad.astype(jnp.float32) + slope * back).astype(jnp.bfloat16)


def tap_terms(act_pad, grad_flat, count):
    frames = act_pad.shape[0] - 2
    rows_here = act_pad.shape[1] - 2
    columns = act_pad.shape[2] - 2
    tap_list = [(i, j, k) for i in range(3) for j in range(3) for k in range(3)]
    per_block = max(1, 128 // count)
    blocks = []
    for tap_start in range(0, 27, per_block):
        pieces = [
            act_pad[i : i + frames, j : j + rows_here, k : k + columns].reshape(-1, count)
            for i, j, k in tap_list[tap_start : tap_start + per_block]
        ]
        stacked = pieces[0]
        blocks.append(
            lax.dot_general(
                stacked, grad_flat, (((0,), (0,)), ((), ())), preferred_element_type=jnp.float32
            )
        )
    joined = jnp.concatenate(blocks, axis=0).reshape(27, count, grad_flat.shape[1])
    return jnp.transpose(joined, (1, 0, 2))


def local(acts, kernels, cotangent):
    frames, rows_here, columns, chans = cotangent.shape
    sections = lax.axis_size("section")
    my_section = lax.axis_index("section")
    groups = lax.axis_size("dp")
    scale = 1.0 / math.sqrt(frames * rows_here * groups * columns)
    share = chans // groups
    xval = acts[0].astype(jnp.float32)
    kern = kernels[0]
    sig = jax.nn.sigmoid(xval)
    slope = sig * (1.0 + xval * (1.0 - sig))
    activ = (xval * sig).astype(jnp.bfloat16)

    def grad_step(padded, grad):
        return grad_update(padded, kern, grad, slope, 1)

    def skip_step(padded, grad):
        return jnp.zeros_like(grad)

    buffer = cotangent
    kept_dx = jnp.zeros_like(cotangent)
    kept_grad = jnp.zeros_like(cotangent)
    for tick in range(sections):
        live = my_section == sections - 1 - tick
        padded = padded_2(buffer, (("dp", 1),), 1)
        result = lax.cond(live, grad_step, skip_step, padded, buffer)
        kept_dx = jnp.where(live, result, kept_dx)
        kept_grad = jnp.where(live, buffer, kept_grad)
        if tick + 1 < sections:
            buffer = shifted(result, "section", -1)
    act_pad = padded_2(activ, (("dp", 1),), 1)
    act_pad = jnp.pad(act_pad, ((2, 0), (0, 0), (1, 1), (0, 0)))
    grad_flat = kept_grad.reshape(-1, chans)
    summed = lax.psum(
        (tap_terms(act_pad, grad_flat, chans) * scale).astype(jnp.bfloat16), "dp"
    ).astype(jnp.float32)
    kernel_part = lax.dynamic_slice_in_dim(summed, lax.axis_index("dp") * share, share, 0)
    return (kept_dx[None], kernel_part[None])


def solution(mesh):
    return jax.shard_map(
        local,
        mesh=mesh,
        in_specs=(
            P("section", None, "dp", None, None),
            P("section", None, None, None, None, None),
            P(None, "dp", None, None),
        ),
        out_specs=(P("section", None, "dp", None, None), P("section", "dp", None, None)),
        check_vma=False,
    )
```

profile of v0, /device:TPU:0, one launch (start us, length us, event | category | flops | bytes accessed | tf_op | source)
XLA Modules:
  0.0 161.0 jit_solution(13595913338648503751)
XLA Ops:
  7.2 1.2 copy.17
  8.7 2.4 %collective-permute-start = (bf16[9,1,32,128]{3,1,2,0:T(2,128)(2,1)S(1)}, bf16[9,1,32,128]{3,1,2,0:T(2,128)(2,1)S(1)}, u32[]{:S(2)}, u32[]{:S(2)}) collective-permute-start(bf16[9,1,32,128]{3,1,2,0:T(2,128)(2,1)S(1)} %get-tuple-element.92), channel_id=1, source_target_pairs={{0,1},{1,2},{2,3},{3,4},{4,5},{5,6},{6,7},{8,9},{9,10},{10,11},{11... | collective-permute-start | bytes 221192 | tf_op jit(solution)/shard_map/ppermute | solution.py:14
  11.1 1.3 collective-permute-start.1
  12.4 1.2 fusion.98
  13.6 2.9 %collective-permute-done.1 = bf16[9,1,32,128]{3,1,2,0:T(2,128)(2,1)S(1)} collective-permute-done((bf16[9,1,32,128]{3,1,2,0:T(2,128)(2,1)S(1)}, bf16[9,1,32,128]{3,1,2,0:T(2,128)(2,1)S(1)}, u32[]{:S(2)}, u32[]{:S(2)}) %collective-permute-start.1) | collective-permute-done | bytes 73760 | tf_op jit(solution)/shard_map/ppermute | solution.py:17
  16.5 0.5 pad_maximum_fusion
  17.1 1.3 collective-permute-start.2
  18.4 7.7 %collective-permute-done.2 = bf16[9,4,32,128]{3,2,1,0:T(8,128)(2,1)S(1)} collective-permute-done((bf16[9,4,32,128]{3,2,1,0:T(8,128)(2,1)S(1)}, bf16[9,4,32,128]{3,2,1,0:T(8,128)(2,1)S(1)}, u32[]{:S(2)}, u32[]{:S(2)}) %collective-permute-start.2) | collective-permute-done | bytes 294944 | tf_op jit(solution)/shard_map/ppermute | solution.py:25
  26.1 4.5 %collective-permute-start.3 = (bf16[9,1,32,128]{3,2,1,0:T(8,128)(2,1)S(1)}, bf16[9,1,32,128]{3,2,1,0:T(8,128)(2,1)S(1)}, u32[]{:S(2)}, u32[]{:S(2)}) collective-permute-start(bf16[9,1,32,128]{3,2,1,0:T(8,128)(2,1)S(1)} %get-tuple-element.90), channel_id=1, source_target_pairs={{0,1},{1,2},{2,3},{3,4},{4,5},{5,6},{6,7},{8,9},{9,10},{10,11},{11... | collective-permute-start | bytes 221192 | tf_op jit(solution)/shard_map/ppermute | solution.py:14
  30.7 1.3 collective-permute-start.4
  32.0 4.2 %collective-permute-done.4 = bf16[9,1,32,128]{3,2,1,0:T(8,128)(2,1)S(1)} collective-permute-done((bf16[9,1,32,128]{3,2,1,0:T(8,128)(2,1)S(1)}, bf16[9,1,32,128]{3,2,1,0:T(8,128)(2,1)S(1)}, u32[]{:S(2)}, u32[]{:S(2)}) %collective-permute-start.4) | collective-permute-done | bytes 73760 | tf_op jit(solution)/shard_map/ppermute | solution.py:17
  36.3 1.3 collective-permute-start.5
  37.6 8.5 %collective-permute-done.5 = bf16[9,4,32,128]{3,2,1,0:T(8,128)(2,1)S(1)} collective-permute-done((bf16[9,4,32,128]{3,2,1,0:T(8,128)(2,1)S(1)}, bf16[9,4,32,128]{3,2,1,0:T(8,128)(2,1)S(1)}, u32[]{:S(2)}, u32[]{:S(2)}) %collective-permute-start.5) | collective-permute-done | bytes 294944 | tf_op jit(solution)/shard_map/ppermute | solution.py:25
  46.1 4.1 %collective-permute-start.6 = (bf16[9,1,32,128]{3,2,1,0:T(8,128)(2,1)S(1)}, bf16[9,1,32,128]{3,2,1,0:T(8,128)(2,1)S(1)}, u32[]{:S(2)}, u32[]{:S(2)}) collective-permute-start(bf16[9,1,32,128]{3,2,1,0:T(8,128)(2,1)S(1)} %get-tuple-element.88), channel_id=1, source_target_pairs={{0,1},{1,2},{2,3},{3,4},{4,5},{5,6},{6,7},{8,9},{9,10},{10,11},{11... | collective-permute-start | bytes 221192 | tf_op jit(solution)/shard_map/ppermute | solution.py:14
  50.2 1.3 collective-permute-start.7
  51.6 3.4 %collective-permute-done.7 = bf16[9,1,32,128]{3,2,1,0:T(8,128)(2,1)S(1)} collective-permute-done((bf16[9,1,32,128]{3,2,1,0:T(8,128)(2,1)S(1)}, bf16[9,1,32,128]{3,2,1,0:T(8,128)(2,1)S(1)}, u32[]{:S(2)}, u32[]{:S(2)}) %collective-permute-start.7) | collective-permute-done | bytes 73760 | tf_op jit(solution)/shard_map/ppermute | solution.py:17
  55.3 1.3 collective-permute-start.8
  56.6 4.9 %collective-permute-start.11 = (bf16[9,1,32,128]{3,2,1,0:T(8,128)(2,1)S(1)}, bf16[9,1,32,128]{3,2,1,0:T(8,128)(2,1)S(1)}, u32[]{:S(2)}, u32[]{:S(2)}) collective-permute-start(bf16[9,1,32,128]{3,2,1,0:T(8,128)(2,1)S(1)} %get-tuple-element.82), channel_id=1, source_target_pairs={{0,1},{1,2},{2,3},{3,4},{4,5},{5,6},{6,7},{8,9},{9,10},{10,11},{11... | collective-permute-start | bytes 221192 | tf_op jit(solution)/shard_map/ppermute | solution.py:14
  61.6 1.3 collective-permute-start.12
  62.9 1.8 %collective-permute-done.12 = bf16[9,1,32,128]{3,2,1,0:T(8,128)(2,1)S(1)} collective-permute-done((bf16[9,1,32,128]{3,2,1,0:T(8,128)(2,1)S(1)}, bf16[9,1,32,128]{3,2,1,0:T(8,128)(2,1)S(1)}, u32[]{:S(2)}, u32[]{:S(2)}) %collective-permute-start.12) | collective-permute-done | bytes 73760 | tf_op jit(solution)/shard_map/ppermute | solution.py:17
  65.0 10.5 %collective-permute-done.8 = bf16[9,4,32,128]{3,2,1,0:T(8,128)(2,1)S(1)} collective-permute-done((bf16[9,4,32,128]{3,2,1,0:T(8,128)(2,1)S(1)}, bf16[9,4,32,128]{3,2,1,0:T(8,128)(2,1)S(1)}, u32[]{:S(2)}, u32[]{:S(2)}) %collective-permute-start.8) | collective-permute-done | bytes 294944 | tf_op jit(solution)/shard_map/ppermute | solution.py:25
  75.5 0.7 fusion.133
  76.2 4.1 %collective-permute-start.9 = (bf16[9,1,32,128]{3,2,1,0:T(8,128)(2,1)}, bf16[9,1,32,128]{3,2,1,0:T(8,128)(2,1)S(1)}, u32[]{:S(2)}, u32[]{:S(2)}) collective-permute-start(bf16[9,1,32,128]{3,2,1,0:T(8,128)(2,1)} %get-tuple-element.86), channel_id=1, source_target_pairs={{0,1},{1,2},{2,3},{3,4},{4,5},{5,6},{6,7},{8,9},{9,10},{10,11},{11... | collective-permute-start | bytes 221192 | tf_op jit(solution)/shard_map/ppermute | solution.py:14
  80.3 1.3 collective-permute-start.10
  89.7 1.1 multiply_convert_fusion
  90.9 5.2 %conditional.7 = (bf16[9,4,32,128]{3,2,1,0:T(8,128)(2,1)S(1)}) conditional(s32[]{:T(128)} %convert_element_type.59, () %tuple.32, (bf16[9,4,32,128]{3,2,1,0:T(8,128)(2,1)S(1)}, bf16[9,6,32,128]{3,2,1,0:T(8,128)(2,1)S(1)}, bf16[3,3,3,128,128]{4,3,2,1,0:T(8,128)(2,1)}, f32[9,4,32,128]{3,2,1,0:T(8,128)S(1)}) %tuple.71), branch_computations={%region_6.7_spmd, %region_7.8_spmd} | conditional | flops 1135558656 | bytes 13114634 | solution.py:88
  91.7 0.8 copy-done.4
  92.5 2.8 %convolution_select_fusion.3 = f32[9,4,8,5,128]{4,2,3,1,0:T(8,128)S(1)} fusion(bf16[3,3,3,128,128]{4,3,2,1,0:T(8,128)(2,1)S(1)} %copy-done.4, bf16[9,6,1,7,2,128]{5,3,4,1,0,2:T(8,128)(2,1)S(1)} %slice.164, bf16[9,6,1,8,5,128]{5,3,4,1,0,2:T(8,128)(2,1)S(1)} %copy.15, pred[8,5]{0,1:T(8,128)(4,1)S(1)} %copy-done.7), kind=kOutput, calls=%fused_computation.52 | convolution fusion | flops 1134968832 | bytes 2368552 | tf_op jit(solution)/shard_map/cond/branch_1_fun/conv_general_dilated | solution.py:30
  95.5 0.6 fusion.51
  96.2 0.8 select_bitcast_fusion
  96.9 55.6 %all-reduce.3.cloned.1.call-done = bf16[128,27,128]{2,0,1:T(8,128)(2,1)} async-done(((bf16[128,27,128]{2,0,1:T(8,128)(2,1)}), bf16[128,27,128]{2,0,1:T(8,128)(2,1)}) %all-reduce.3.cloned.1.call-update) | async-done | bytes 884752 | tf_op jit(solution)/shard_map/psum | solution.py:96
  152.5 1.6 convert_bitcast_fusion
  (65 shorter events, 10.0 us)
Async XLA Ops:
  7.2 9.9 %copy-start = (bf16[9,4,32,128]{3,2,1,0:T(8,128)(2,1)S(1)}, bf16[9,4,32,128]{3,2,1,0:T(8,128)(2,1)}, u32[]{:S(2)}) copy-start(bf16[9,4,32,128]{3,2,1,0:T(8,128)(2,1)} %param.13) | copy-start | bytes 884740
  7.2 9.9 %copy-start.2 = (bf16[1,3,3,3,128,128]{5,4,3,2,1,0:T(8,128)(2,1)S(1)}, bf16[1,3,3,3,128,128]{5,4,3,2,1,0:T(8,128)(2,1)}, u32[]{:S(2)}) copy-start(bf16[1,3,3,3,128,128]{5,4,3,2,1,0:T(8,128)(2,1)} %param.12) | copy-start | bytes 2654212
  7.2 145.4 %all-reduce.3.cloned.1.call-start = ((), (), s32[]{:S(2)}) async-start(), calls=%async_computation | async-start | bytes 1769472 | tf_op jit(solution)/shard_map/psum | solution.py:96
  8.7 4.9 %collective-permute-start = (bf16[9,1,32,128]{3,1,2,0:T(2,128)(2,1)S(1)}, bf16[9,1,32,128]{3,1,2,0:T(2,128)(2,1)S(1)}, u32[]{:S(2)}, u32[]{:S(2)}) collective-permute-start(bf16[9,1,32,128]{3,1,2,0:T(2,128)(2,1)S(1)} %get-tuple-element.92), channel_id=1, source_target_pairs={{0,1},{1,2},{2,3},{3,4},{4,5},{5,6},{6,7},{8,9},{9,10},{10,11},{11... | collective-permute-start | bytes 221192 | tf_op jit(solution)/shard_map/ppermute | solution.py:14
  11.1 5.4 %collective-permute-start.1 = (bf16[9,1,32,128]{3,1,2,0:T(2,128)(2,1)S(1)}, bf16[9,1,32,128]{3,1,2,0:T(2,128)(2,1)S(1)}, u32[]{:S(2)}, u32[]{:S(2)}) collective-permute-start(bf16[9,1,32,128]{3,1,2,0:T(2,128)(2,1)S(1)} %get-tuple-element.93), channel_id=1, source_target_pairs={{1,0},{2,1},{3,2},{4,3},{5,4},{6,5},{7,6},{9,8},{10,9},{11,10},{12... | collective-permute-start | bytes 221192 | tf_op jit(solution)/shard_map/ppermute | solution.py:17
  17.1 9.0 %collective-permute-start.2 = (bf16[9,4,32,128]{3,2,1,0:T(8,128)(2,1)S(1)}, bf16[9,4,32,128]{3,2,1,0:T(8,128)(2,1)S(1)}, u32[]{:S(2)}, u32[]{:S(2)}) collective-permute-start(bf16[9,4,32,128]{3,2,1,0:T(8,128)(2,1)S(1)} %get-tuple-element.78), channel_id=1, source_target_pairs={{8,0},{16,8},{24,16},{9,1},{17,9},{25,17},{10,2},{18,10},{26,18},{... | collective-permute-start | bytes 884744 | tf_op jit(solution)/shard_map/ppermute | solution.py:25
  26.1 5.8 %collective-permute-start.3 = (bf16[9,1,32,128]{3,2,1,0:T(8,128)(2,1)S(1)}, bf16[9,1,32,128]{3,2,1,0:T(8,128)(2,1)S(1)}, u32[]{:S(2)}, u32[]{:S(2)}) collective-permute-start(bf16[9,1,32,128]{3,2,1,0:T(8,128)(2,1)S(1)} %get-tuple-element.90), channel_id=1, source_target_pairs={{0,1},{1,2},{2,3},{3,4},{4,5},{5,6},{6,7},{8,9},{9,10},{10,11},{11... | collective-permute-start | bytes 221192 | tf_op jit(solution)/shard_map/ppermute | solution.py:14
  30.7 5.5 %collective-permute-start.4 = (bf16[9,1,32,128]{3,2,1,0:T(8,128)(2,1)S(1)}, bf16[9,1,32,128]{3,2,1,0:T(8,128)(2,1)S(1)}, u32[]{:S(2)}, u32[]{:S(2)}) collective-permute-start(bf16[9,1,32,128]{3,2,1,0:T(8,128)(2,1)S(1)} %get-tuple-element.91), channel_id=1, source_target_pairs={{1,0},{2,1},{3,2},{4,3},{5,4},{6,5},{7,6},{9,8},{10,9},{11,10},{12... | collective-permute-start | bytes 221192 | tf_op jit(solution)/shard_map/ppermute | solution.py:17
  36.3 9.8 %collective-permute-start.5 = (bf16[9,4,32,128]{3,2,1,0:T(8,128)(2,1)S(1)}, bf16[9,4,32,128]{3,2,1,0:T(8,128)(2,1)S(1)}, u32[]{:S(2)}, u32[]{:S(2)}) collective-permute-start(bf16[9,4,32,128]{3,2,1,0:T(8,128)(2,1)S(1)} %get-tuple-element.79), channel_id=1, source_target_pairs={{8,0},{16,8},{24,16},{9,1},{17,9},{25,17},{10,2},{18,10},{26,18},{... | collective-permute-start | bytes 884744 | tf_op jit(solution)/shard_map/ppermute | solution.py:25
  46.1 5.4 %collective-permute-start.6 = (bf16[9,1,32,128]{3,2,1,0:T(8,128)(2,1)S(1)}, bf16[9,1,32,128]{3,2,1,0:T(8,128)(2,1)S(1)}, u32[]{:S(2)}, u32[]{:S(2)}) collective-permute-start(bf16[9,1,32,128]{3,2,1,0:T(8,128)(2,1)S(1)} %get-tuple-element.88), channel_id=1, source_target_pairs={{0,1},{1,2},{2,3},{3,4},{4,5},{5,6},{6,7},{8,9},{9,10},{10,11},{11... | collective-permute-start | bytes 221192 | tf_op jit(solution)/shard_map/ppermute | solution.py:14
  50.2 4.7 %collective-permute-start.7 = (bf16[9,1,32,128]{3,2,1,0:T(8,128)(2,1)S(1)}, bf16[9,1,32,128]{3,2,1,0:T(8,128)(2,1)S(1)}, u32[]{:S(2)}, u32[]{:S(2)}) collective-permute-start(bf16[9,1,32,128]{3,2,1,0:T(8,128)(2,1)S(1)} %get-tuple-element.89), channel_id=1, source_target_pairs={{1,0},{2,1},{3,2},{4,3},{5,4},{6,5},{7,6},{9,8},{10,9},{11,10},{12... | collective-permute-start | bytes 221192 | tf_op jit(solution)/shard_map/ppermute | solution.py:17
  55.3 20.2 %collective-permute-start.8 = (bf16[9,4,32,128]{3,2,1,0:T(8,128)(2,1)S(1)}, bf16[9,4,32,128]{3,2,1,0:T(8,128)(2,1)S(1)}, u32[]{:S(2)}, u32[]{:S(2)}) collective-permute-start(bf16[9,4,32,128]{3,2,1,0:T(8,128)(2,1)S(1)} %get-tuple-element.80), channel_id=1, source_target_pairs={{8,0},{16,8},{24,16},{9,1},{17,9},{25,17},{10,2},{18,10},{26,18},{... | collective-permute-start | bytes 884744 | tf_op jit(solution)/shard_map/ppermute | solution.py:25
  56.6 6.2 %collective-permute-start.11 = (bf16[9,1,32,128]{3,2,1,0:T(8,128)(2,1)S(1)}, bf16[9,1,32,128]{3,2,1,0:T(8,128)(2,1)S(1)}, u32[]{:S(2)}, u32[]{:S(2)}) collective-permute-start(bf16[9,1,32,128]{3,2,1,0:T(8,128)(2,1)S(1)} %get-tuple-element.82), channel_id=1, source_target_pairs={{0,1},{1,2},{2,3},{3,4},{4,5},{5,6},{6,7},{8,9},{9,10},{10,11},{11... | collective-permute-start | bytes 221192 | tf_op jit(solution)/shard_map/ppermute | solution.py:14
  61.6 3.2 %collective-permute-start.12 = (bf16[9,1,32,128]{3,2,1,0:T(8,128)(2,1)S(1)}, bf16[9,1,32,128]{3,2,1,0:T(8,128)(2,1)S(1)}, u32[]{:S(2)}, u32[]{:S(2)}) collective-permute-start(bf16[9,1,32,128]{3,2,1,0:T(8,128)(2,1)S(1)} %get-tuple-element.83), channel_id=1, source_target_pairs={{1,0},{2,1},{3,2},{4,3},{5,4},{6,5},{7,6},{9,8},{10,9},{11,10},{12... | collective-permute-start | bytes 221192 | tf_op jit(solution)/shard_map/ppermute | solution.py:17
  76.2 14.7 %collective-permute-start.9 = (bf16[9,1,32,128]{3,2,1,0:T(8,128)(2,1)}, bf16[9,1,32,128]{3,2,1,0:T(8,128)(2,1)S(1)}, u32[]{:S(2)}, u32[]{:S(2)}) collective-permute-start(bf16[9,1,32,128]{3,2,1,0:T(8,128)(2,1)} %get-tuple-element.86), channel_id=1, source_target_pairs={{0,1},{1,2},{2,3},{3,4},{4,5},{5,6},{6,7},{8,9},{9,10},{10,11},{11... | collective-permute-start | bytes 221192 | tf_op jit(solution)/shard_map/ppermute | solution.py:14
  80.3 10.6 %collective-permute-start.10 = (bf16[9,1,32,128]{3,2,1,0:T(8,128)(2,1)}, bf16[9,1,32,128]{3,2,1,0:T(8,128)(2,1)S(1)}, u32[]{:S(2)}, u32[]{:S(2)}) collective-permute-start(bf16[9,1,32,128]{3,2,1,0:T(8,128)(2,1)} %get-tuple-element.87), channel_id=1, source_target_pairs={{1,0},{2,1},{3,2},{4,3},{5,4},{6,5},{7,6},{9,8},{10,9},{11,10},{12... | collective-permute-start | bytes 221192 | tf_op jit(solution)/shard_map/ppermute | solution.py:17
  87.2 1.0 copy-start.1
  91.3 1.2 copy-start.4
  91.4 1.2 copy-start.7
Sparse Core Ops, SparseCore 0:
  90.9 61.5 all-reduce.2
where the time goes:
time: 162 us; the launch traced here: 161 us
  waiting for transfers between devices  94.7 us (58%)
  starting transfers between devices  30.4 us (19%)
  between operations  14.5 us (9%)
  matrix products  10.6 us (7%)
  other arithmetic  6.18 us (4%)
  local copies, waits for them, and re-layouts  3.97 us (2%)
    psum x1, waiting for transfers between devices, local(): lax.psum((tap_terms(act_pad, grad_flat, chans) * scale).astype(jnp.bfloat...  55.6 us
    ppermute x3, waiting for transfers between devices, shifted(): return lax.ppermute(block, axis, route)  26.7 us
    ppermute x5, starting transfers between devices, padded_2(): lax.ppermute(lax.slice_in_dim(block, block.shape[dim] - width, None, axis...  20 us
    ppermute x5, waiting for transfers between devices, padded_2(): lax.ppermute(lax.slice_in_dim(block, 0, width, axis=dim), axis, backward)  12.4 us
    dot_general x27, matrix products, tap_terms(): lax.dot_general(stacked, grad_flat, (((0,), (0,)), ((), ())), preferred_e...  7.8 us
    ppermute x5, starting transfers between devices, padded_2(): lax.ppermute(lax.slice_in_dim(block, 0, width, axis=dim), axis, backward)  6.46 us
    ppermute x3, starting transfers between devices, shifted(): return lax.ppermute(block, axis, route)  3.88 us
  transfers between devices with their start and end apart: 14, of which 8 were waited for; matrix products, arithmetic and copies ran while one was open for 10% of the time, Pallas kernels for 0%

commit v1 on v0

v1 whole, which is shorter than its diff:
```python
import functools
import math

import jax
import jax.numpy as jnp
from jax import lax
from jax.experimental import pallas as pl
from jax.experimental.pallas import tpu as pltpu
from jax.sharding import PartitionSpec as P

MESH = pl.DeviceIdType.MESH
F32 = jnp.float32
BF16 = jnp.bfloat16


def kernel(
    S, G, step, share,
    acts, kern, cot,
    dx, dw,
    gp, g9, kt, slope, ut, acc, sb, r1, c2, r2,
    main_s, main_r, lo_s, lo_r, hi_s, hi_r, lo_c, hi_c, s1, q1, s2, q2,
):
    F, R, W, C = cot.shape
    Z = G // 2
    n = step
    M = n * R * W
    chunks = F // n
    s = lax.axis_index("section")
    d = lax.axis_index("dp")
    z = d // 2
    core = d % 2
    first = s == S - 1
    prev, nxt = jnp.maximum(s - 1, 0), jnp.minimum(s + 1, S - 1)
    below, above = jnp.maximum(d - 1, 0), jnp.minimum(d + 1, G - 1)
    partner = d + 1 - 2 * core
    has_below, has_above = d > 0, d < G - 1
    has_prev, has_next = s > 0, s < S - 1

    barrier = pltpu.get_barrier_semaphore()

    def greet(sec, dev):
        pl.semaphore_signal(barrier, inc=1, device_id=(sec, dev), device_id_type=MESH)

    def greet_three(sec, own):
        if own:
            greet(sec, d)

        @pl.when(has_below)
        def _():
            greet(sec, below)

        @pl.when(has_above)
        def _():
            greet(sec, above)

    greet_three(s, False)

    @pl.when(has_prev)
    def _():
        greet_three(prev, True)

    @pl.when(has_next)
    def _():
        greet_three(nxt, True)

    for zz in range(Z):
        @pl.when(z != zz)
        def _():
            greet(s, 2 * zz + core)

    ends = has_below.astype(jnp.int32) + has_above.astype(jnp.int32)
    sides = has_prev.astype(jnp.int32) + has_next.astype(jnp.int32)
    pl.semaphore_wait(barrier, ends + sides * (ends + 1) + (Z - 1))

    def rows_copy(q):
        f = pl.ds(q * n, n)
        return pltpu.make_async_remote_copy(
            dx.at[f], gp.at[f, pl.ds(1, R)], main_s.at[q], main_r.at[q],
            device_id=(prev, d), device_id_type=MESH)

    def low_copy(q, source, sec, sent):
        f = pl.ds(q * n, n)
        return pltpu.make_async_remote_copy(
            source.at[f, pl.ds(R - 1, 1)], gp.at[f, pl.ds(0, 1)], sent.at[q], lo_r.at[q],
            device_id=(sec, above), device_id_type=MESH)

    def high_copy(q, source, sec, sent):
        f = pl.ds(q * n, n)
        return pltpu.make_async_remote_copy(
            source.at[f, pl.ds(0, 1)], gp.at[f, pl.ds(R + 1, 1)], sent.at[q], hi_r.at[q],
            device_id=(sec, below), device_id_type=MESH)

    def start_edges(q, source, sec, low_sent, high_sent):
        @pl.when(has_above)
        def _():
            low_copy(q, source, sec, low_sent).start()

        @pl.when(has_below)
        def _():
            high_copy(q, source, sec, high_sent).start()

    order = list(range(chunks))[::-1]

    @pl.when(first)
    def _():
        for q in order:
            start_edges(q, cot, s, lo_c, hi_c)
        gp[pl.ds(0, F), pl.ds(1, R)] = cot[...]

    gp[pl.ds(F, 2)] = jnp.zeros((2, R + 2, W, C), BF16)

    @pl.when(d == 0)
    def _():
        gp[pl.ds(0, F), pl.ds(0, 1)] = jnp.zeros((F, 1, W, C), BF16)

    @pl.when(d == G - 1)
    def _():
        gp[pl.ds(0, F), pl.ds(R + 1, 1)] = jnp.zeros((F, 1, W, C), BF16)

    for i in range(3):
        for j in range(3):
            for k in range(3):
                kt[pl.ds((3 * i + j) * C, C), pl.ds(k * C, C)] = kern[i, j, k].T

    col = lax.rem(lax.broadcasted_iota(jnp.int32, (M, C), 0), W)
    not_first, not_last = col > 0, col < W - 1

    def from_left(v):
        return jnp.where(not_first, pltpu.roll(v, 1, 0), 0.0)

    def from_right(v):
        return jnp.where(not_last, pltpu.roll(v, M - 1, 0), 0.0)

    for q in order:
        x = acts[pl.ds(q * n, n)].reshape(M, C).astype(F32)
        sig = jax.nn.sigmoid(x)
        slope[pl.ds(q * M, M)] = sig * (1.0 + x * (1.0 - sig))
        u = (x * sig).astype(BF16).astype(F32)
        for k, v in enumerate((from_left(u), u, from_right(u))):
            ut[pl.ds(k * C, C), pl.ds(q * M, M)] = v.T.astype(BF16)

    def share_out(i, part):
        for j in range(3):
            for k in range(3):
                block = part[k * C:(k + 1) * C, j * C:(j + 1) * C].astype(BF16)
                if share % 16 == 0:
                    block = block.reshape(Z, 2, share, C)
                    for p in range(2):
                        sb[i, p, :, 3 * j + k] = block[:, p]
                else:
                    for dd in range(G):
                        sb[i, dd % 2, dd // 2, 3 * j + k, pl.ds(0, share)] = (
                            block[dd * share:(dd + 1) * share])

    def pair_copy(i):
        return pltpu.make_async_remote_copy(
            sb.at[i, 1 - core], r1.at[i], s1.at[i], q1.at[i],
            device_id=(s, partner), device_id_type=MESH)

    def chip_copy(i, zz):
        return pltpu.make_async_remote_copy(
            c2.at[i, zz], r2.at[i, z], s2.at[i, zz], q2.at[i, z],
            device_id=(s, 2 * zz + core), device_id_type=MESH)

    def chip_arrival(i, zz):
        return pltpu.make_async_remote_copy(
            c2.at[i, zz], r2.at[i, zz], s2.at[i, zz], q2.at[i, zz],
            device_id=(s, 2 * zz + core), device_id_type=MESH)

    for q in order:
        f = pl.ds(q * n, n)

        @pl.when(has_next)
        def _():
            rows_copy(q).wait_recv()

        @pl.when(has_below)
        def _():
            low_copy(q, dx, prev, lo_s).wait_recv()

        @pl.when(has_above)
        def _():
            high_copy(q, dx, prev, hi_s).wait_recv()

        for i in range(3):
            for j in range(3):
                g9[:, pl.ds((3 * i + j) * C, C)] = gp[
                    pl.ds(q * n + 2 - i, n), pl.ds(2 - j, R)].reshape(M, C)

        parts = jnp.dot(g9[...], kt[...], preferred_element_type=F32)
        back = from_right(parts[:, :C]) + parts[:, C:2 * C] + from_left(parts[:, 2 * C:])
        g = gp[f, pl.ds(1, R)].reshape(M, C).astype(F32)
        dx[f] = (g + slope[pl.ds(q * M, M)] * back).astype(BF16).reshape(n, R, W, C)

        @pl.when(has_prev)
        def _():
            start_edges(q, dx, prev, lo_s, hi_s)
            rows_copy(q).start()

        for i in range(3):
            cols = pl.ds(i * 3 * C, 3 * C)
            term = jnp.dot(ut[:, pl.ds(q * M, M)], g9[:, cols], preferred_element_type=F32)
            if q != order[0]:
                term = acc[:, cols] + term
            if q != order[-1]:
                acc[:, cols] = term
            else:
                share_out(i, term)
                pair_copy(i).start()

    for i in range(3):
        pair_copy(i).wait_recv()
        c2[i] = (sb[i, core].astype(F32) + r1[i].astype(F32)).astype(BF16)
        for zz in range(Z):
            @pl.when(z != zz)
            def _():
                chip_copy(i, zz).start()
        r2[i, z] = c2[i, z]

    for i in range(3):
        for zz in range(Z):
            @pl.when(z != zz)
            def _():
                chip_arrival(i, zz).wait_recv()
        total = r2[i, 0].astype(F32)
        for zz in range(1, Z):
            total = total + r2[i, zz].astype(F32)
        dw[pl.ds(9 * i, 9)] = total

    for i in range(3):
        pair_copy(i).wait_send()
        for zz in range(Z):
            @pl.when(z != zz)
            def _():
                chip_copy(i, zz).wait_send()

    for q in order:
        @pl.when(has_prev)
        def _():
            rows_copy(q).wait_send()

        @pl.when(has_above & has_prev)
        def _():
            low_copy(q, dx, prev, lo_s).wait_send()

        @pl.when(has_below & has_prev)
        def _():
            high_copy(q, dx, prev, hi_s).wait_send()

        @pl.when(has_above & first)
        def _():
            low_copy(q, cot, s, lo_c).wait_send()

        @pl.when(has_below & first)
        def _():
            high_copy(q, cot, s, hi_c).wait_send()


def local(S, G, acts, kernels, cotangent):
    F, R, W, C = cotangent.shape
    share = C // G
    sp = -(-share // 16) * 16
    Z = G // 2
    step = 3 if F % 3 == 0 else 1
    chunks = F // step
    scale = 1.0 / math.sqrt(F * R * G * W)
    dma = pltpu.SemaphoreType.DMA
    dx, dw = pl.pallas_call(
        functools.partial(kernel, S, G, step, share),
        out_shape=(
            jax.ShapeDtypeStruct((F, R, W, C), BF16),
            jax.ShapeDtypeStruct((27, sp, C), F32),
        ),
        in_specs=[pl.BlockSpec(memory_space=pltpu.VMEM)] * 3,
        out_specs=[pl.BlockSpec(memory_space=pltpu.VMEM)] * 2,
        scratch_shapes=[
            pltpu.VMEM((F + 2, R + 2, W, C), BF16),
            pltpu.VMEM((step * R * W, 9 * C), BF16),
            pltpu.VMEM((9 * C, 3 * C), BF16),
            pltpu.VMEM((F * R * W, C), F32),
            pltpu.VMEM((3 * C, F * R * W), BF16),
            pltpu.VMEM((3 * C, 9 * C), F32),
            pltpu.VMEM((3, 2, Z, 9, sp, C), BF16),
            pltpu.VMEM((3, Z, 9, sp, C), BF16),
            pltpu.VMEM((3, Z, 9, sp, C), BF16),
            pltpu.VMEM((3, Z, 9, sp, C), BF16),
            dma((chunks,)), dma((chunks,)), dma((chunks,)), dma((chunks,)),
            dma((chunks,)), dma((chunks,)), dma((chunks,)), dma((chunks,)),
            dma((3,)), dma((3,)), dma((3, Z)), dma((3, Z)),
        ],
        compiler_params=pltpu.CompilerParams(
            collective_id=0, has_side_effects=True, vmem_limit_bytes=48 * 2**20
        ),
        cost_estimate=pl.CostEstimate(
            flops=4 * 27 * F * R * W * C * C, bytes_accessed=4 * 27 * C * C, transcendentals=F * R * W * C
        ),
    )(acts[0], kernels[0], cotangent)
    kernel_part = jnp.transpose(dw[:, :share], (1, 0, 2)) * scale
    return (dx[None], kernel_part[None])


def solution(mesh):
    return jax.shard_map(
        functools.partial(local, mesh.shape["section"], mesh.shape["dp"]),
        mesh=mesh,
        in_specs=(
            P("section", None, "dp", None, None),
            P("section", None, None, None, None, None),
            P(None, "dp", None, None),
        ),
        out_specs=(P("section", None, "dp", None, None), P("section", "dp", None, None)),
        check_vma=False,
    )
```

time: 162 us -> 50.5 us (0.31)
  waiting for transfers between devices: 94.7 us -> 0 us
  Pallas kernels: 0 us -> 45.1 us
  starting transfers between devices: 30.4 us -> 0 us
  between operations: 14.5 us -> 0.65 us
  matrix products: 10.6 us -> 0 us
  other arithmetic: 6.18 us -> 0.71 us
    psum x1 -> x0, waiting for transfers between devices: 55.6 us -> none  [local(): lax.psum((tap_terms(act_pad, grad_flat, chans) * scale).astype(jnp.bfloat...]
    pallas_call x0 -> x1, Pallas kernels: none -> 45.1 us  [local(): pl.pallas_call(functools.partial(kernel, S, G, step, share), out_shape=(j...]
    ppermute x13 -> x0, waiting for transfers between devices: 39.1 us -> none  [the longest x3 26.7 us: shifted(): return lax.ppermute(block, axis, route)]
    ppermute x13 -> x0, starting transfers between devices: 30.4 us -> none  [the longest x5 20 us: padded_2(): lax.ppermute(lax.slice_in_dim(block, block.shape[dim] - width, None, axis...]
    dot_general x27 -> x0, matrix products: 7.8 us -> none  [tap_terms(): lax.dot_general(stacked, grad_flat, (((0,), (0,)), ((), ())), preferred_e...]
    convert_element_type x3 -> x0, other arithmetic: 2.85 us -> none  [the longest x1 1.23 us: local(): activ = (xval * sig).astype(jnp.bfloat16)]
    conv_general_dilated x1 -> x0, matrix products: 2.8 us -> none  [grad_update(): lax.conv_general_dilated(padded[None], flipped, (1, 1, 1), ((0, 2), (0, 0...]
    unnamed x7, local copies, waits for them, and re-layouts: 1.29 us -> 3.8 us
  transfers between devices with their start and end apart: 14 -> 0, of which waited for: 8 -> 0; matrix products, arithmetic and copies ran while one was open for 10% -> 0% of each run, Pallas kernels for 0% -> 0%
where the time goes in v1:
time: 50.5 us; the launch traced here: 50.3 us
  Pallas kernels  45.1 us (89%)
  local copies, waits for them, and re-layouts  3.8 us (8%)
  other arithmetic  0.71 us (1%)
  between operations  0.65 us (1%)
    pallas_call x1, Pallas kernels, local(): pl.pallas_call(functools.partial(kernel, S, G, step, share), out_shape=(j...  45.1 us
    unnamed x7, local copies, waits for them, and re-layouts  3.8 us

profile of v1, /device:TPU:0, one launch (start us, length us, event | category | flops | bytes accessed | tf_op | source)
XLA Modules:
  0.0 50.3 jit_solution(5937283126912789023)
XLA Ops:
  0.6 0.0 copy-start
  0.6 1.2 %copy-done = bf16[1,3,3,3,128,128]{5,4,3,2,1,0:T(8,128)(2,1)S(1)} copy-done((bf16[1,3,3,3,128,128]{5,4,3,2,1,0:T(8,128)(2,1)S(1)}, bf16[1,3,3,3,128,128]{5,4,3,2,1,0:T(8,128)(2,1)}, u32[]{:S(2)}) %copy-start) | copy-done | bytes 884760
  1.8 0.0 copy-start.1
  1.8 1.0 %copy-done.1 = bf16[1,9,4,32,128]{4,3,2,1,0:T(8,128)(2,1)S(1)} copy-done((bf16[1,9,4,32,128]{4,3,2,1,0:T(8,128)(2,1)S(1)}, bf16[1,9,4,32,128]{4,3,2,1,0:T(8,128)(2,1)}, u32[]{:S(2)}) %copy-start.1) | copy-done | bytes 294936
  2.8 0.0 copy-start.2
  2.8 1.0 %copy-done.2 = bf16[9,4,32,128]{3,2,1,0:T(8,128)(2,1)S(1)} copy-done((bf16[9,4,32,128]{3,2,1,0:T(8,128)(2,1)S(1)}, bf16[9,4,32,128]{3,2,1,0:T(8,128)(2,1)}, u32[]{:S(2)}) %copy-start.2) | copy-done | bytes 294936
  3.7 45.1 %shard_map.50 = (bf16[9,4,32,128]{3,2,1,0:T(8,128)(2,1)S(1)}, f32[27,16,128]{2,1,0:T(8,128)S(1)}) custom-call(bf16[9,4,32,128]{3,2,1,0:T(8,128)(2,1)S(1)} %bitcast.9, bf16[3,3,3,128,128]{4,3,2,1,0:T(8,128)(2,1)S(1)} %bitcast.8, bf16[9,4,32,128]{3,2,1,0:T(8,128)(2,1)S(1)} %copy-done.2), custom_call_target="tpu_custom_call" | custom-call | flops 2038431744 | bytes 1769472 | tf_op jit(solution)/shard_map/pallas_call | solution.py:268
  48.9 0.7 %multiply_bitcast_fusion = f32[1,16,27,128]{3,1,2,0:T(8,128)} fusion(f32[27,16,128]{2,1,0:T(8,128)S(1)} %get-tuple-element.5), kind=kLoop, calls=%fused_computation | loop fusion | flops 55296 | bytes 442368 | tf_op jit(solution)/shard_map/broadcast_in_dim | solution.py:299
  49.6 0.7 %copy.6 = bf16[1,9,4,32,128]{4,3,2,1,0:T(8,128)(2,1)} copy(bf16[1,9,4,32,128]{4,3,2,1,0:T(8,128)(2,1)S(1)} %bitcast.7) | data formatting | bytes 589824
Async XLA Ops:
  0.6 1.2 %copy-start = (bf16[1,3,3,3,128,128]{5,4,3,2,1,0:T(8,128)(2,1)S(1)}, bf16[1,3,3,3,128,128]{5,4,3,2,1,0:T(8,128)(2,1)}, u32[]{:S(2)}) copy-start(bf16[1,3,3,3,128,128]{5,4,3,2,1,0:T(8,128)(2,1)} %param.4) | copy-start | bytes 2654212
  1.8 1.0 %copy-start.1 = (bf16[1,9,4,32,128]{4,3,2,1,0:T(8,128)(2,1)S(1)}, bf16[1,9,4,32,128]{4,3,2,1,0:T(8,128)(2,1)}, u32[]{:S(2)}) copy-start(bf16[1,9,4,32,128]{4,3,2,1,0:T(8,128)(2,1)} %param.3) | copy-start | bytes 884740
  2.8 1.0 %copy-start.2 = (bf16[9,4,32,128]{3,2,1,0:T(8,128)(2,1)S(1)}, bf16[9,4,32,128]{3,2,1,0:T(8,128)(2,1)}, u32[]{:S(2)}) copy-start(bf16[9,4,32,128]{3,2,1,0:T(8,128)(2,1)} %cot.1) | copy-start | bytes 884740

commit v2 on v1

v2 whole, which is shorter than its diff:
```python
import functools
import math

import jax
import jax.numpy as jnp
from jax import lax
from jax.experimental import pallas as pl
from jax.experimental.pallas import tpu as pltpu
from jax.sharding import PartitionSpec as P

MESH = pl.DeviceIdType.MESH
F32 = jnp.float32
BF16 = jnp.bfloat16


def kernel(
    S, G, share,
    acts_h, kern_h, cot_h,
    dx, dw,
    acts, kern, gp, g9, kt, slope, ut, acc, sb, r1, c2, r2,
    main_s, main_r, lo_s, lo_r, hi_s, hi_r, edge_s, edge_r, load, s1, q1, s2, q2,
):
    F, R, W, C = cot_h.shape
    Z = G // 2
    M = R * W
    N = 3 * C
    s = lax.axis_index("section")
    d = lax.axis_index("dp")
    z = d // 2
    core = d % 2
    first = s == S - 1
    prev, nxt = jnp.maximum(s - 1, 0), jnp.minimum(s + 1, S - 1)
    below, above = jnp.maximum(d - 1, 0), jnp.minimum(d + 1, G - 1)
    partner = d + 1 - 2 * core
    has_below, has_above = d > 0, d < G - 1
    has_prev, has_next = s > 0, s < S - 1

    acts_load = pltpu.make_async_copy(acts_h, acts, load.at[0])
    kern_load = pltpu.make_async_copy(kern_h, kern, load.at[1])
    cot_load = pltpu.make_async_copy(cot_h, gp.at[:, pl.ds(1, R)], load.at[2])
    acts_load.start()
    kern_load.start()

    @pl.when(first)
    def _():
        cot_load.start()

    barrier = pltpu.get_barrier_semaphore()

    def greet(sec, dev):
        pl.semaphore_signal(barrier, inc=1, device_id=(sec, dev), device_id_type=MESH)

    def greet_three(sec, own):
        if own:
            greet(sec, d)

        @pl.when(has_below)
        def _():
            greet(sec, below)

        @pl.when(has_above)
        def _():
            greet(sec, above)

    greet_three(s, False)

    @pl.when(has_prev)
    def _():
        greet_three(prev, True)

    @pl.when(has_next)
    def _():
        greet_three(nxt, True)

    for zz in range(Z):
        @pl.when(z != zz)
        def _():
            greet(s, 2 * zz + core)

    acts_load.wait()
    for t in range(F):
        x = acts[t].reshape(M, C).astype(F32)
        sig = jax.nn.sigmoid(x)
        slope[t] = sig * (1.0 + x * (1.0 - sig))

    ends = has_below.astype(jnp.int32) + has_above.astype(jnp.int32)
    sides = has_prev.astype(jnp.int32) + has_next.astype(jnp.int32)
    pl.semaphore_wait(barrier, ends + sides * (ends + 1) + (Z - 1))

    def cot_low():
        return pltpu.make_async_remote_copy(
            cot_h.at[:, pl.ds(R - 1, 1)], gp.at[:, pl.ds(0, 1)], edge_s.at[0], edge_r.at[0],
            device_id=(s, above), device_id_type=MESH)

    def cot_high():
        return pltpu.make_async_remote_copy(
            cot_h.at[:, pl.ds(0, 1)], gp.at[:, pl.ds(R + 1, 1)], edge_s.at[1], edge_r.at[1],
            device_id=(s, below), device_id_type=MESH)

    def rows_copy(t):
        return pltpu.make_async_remote_copy(
            dx.at[t], gp.at[t, pl.ds(1, R)], main_s.at[t], main_r.at[t],
            device_id=(prev, d), device_id_type=MESH)

    def low_copy(t):
        return pltpu.make_async_remote_copy(
            dx.at[t, pl.ds(R - 1, 1)], gp.at[t, pl.ds(0, 1)], lo_s.at[t], lo_r.at[t],
            device_id=(prev, above), device_id_type=MESH)

    def high_copy(t):
        return pltpu.make_async_remote_copy(
            dx.at[t, pl.ds(0, 1)], gp.at[t, pl.ds(R + 1, 1)], hi_s.at[t], hi_r.at[t],
            device_id=(prev, below), device_id_type=MESH)

    @pl.when(first & has_above)
    def _():
        cot_low().start()

    @pl.when(first & has_below)
    def _():
        cot_high().start()

    @pl.when(d == 0)
    def _():
        gp[:, pl.ds(0, 1)] = jnp.zeros((F, 1, W, C), BF16)

    @pl.when(d == G - 1)
    def _():
        gp[:, pl.ds(R + 1, 1)] = jnp.zeros((F, 1, W, C), BF16)

    g9[F - 1, :, pl.ds(0, 2 * N)] = jnp.zeros((M, 2 * N), BF16)
    g9[F - 2, :, pl.ds(0, N)] = jnp.zeros((M, N), BF16)

    kern_load.wait()
    for i in range(3):
        for j in range(3):
            for k in range(3):
                kt[pl.ds((3 * i + j) * C, C), pl.ds(k * C, C)] = kern[i, j, k].T

    col = lax.rem(lax.broadcasted_iota(jnp.int32, (M, C), 0), W)
    not_first, not_last = col > 0, col < W - 1

    def from_left(v):
        return jnp.where(not_first, pltpu.roll(v, 1, 0), 0.0)

    def from_right(v):
        return jnp.where(not_last, pltpu.roll(v, M - 1, 0), 0.0)

    def activated():
        for t in range(F):
            x = acts[t].reshape(M, C).astype(F32)
            u = (x * jax.nn.sigmoid(x)).astype(BF16).astype(F32)
            for k, v in enumerate((from_left(u), u, from_right(u))):
                ut[pl.ds(k * C, C), pl.ds(t * M, M)] = v.T.astype(BF16)

    pl.when(has_next)(activated)

    def share_out(i, part):
        for j in range(3):
            for k in range(3):
                block = part[k * C:(k + 1) * C, j * C:(j + 1) * C].astype(BF16)
                if share % 16 == 0:
                    block = block.reshape(Z, 2, share, C)
                    for p in range(2):
                        sb[i, p, :, 3 * j + k] = block[:, p]
                else:
                    for dd in range(G):
                        sb[i, dd % 2, dd // 2, 3 * j + k, pl.ds(0, share)] = (
                            block[dd * share:(dd + 1) * share])

    def pair_copy(i):
        return pltpu.make_async_remote_copy(
            sb.at[i, 1 - core], r1.at[i], s1.at[i], q1.at[i],
            device_id=(s, partner), device_id_type=MESH)

    def chip_copy(i, zz):
        return pltpu.make_async_remote_copy(
            c2.at[i, zz], r2.at[i, z], s2.at[i, zz], q2.at[i, z],
            device_id=(s, 2 * zz + core), device_id_type=MESH)

    def chip_arrival(i, zz):
        return pltpu.make_async_remote_copy(
            c2.at[i, zz], r2.at[i, zz], s2.at[i, zz], q2.at[i, zz],
            device_id=(s, 2 * zz + core), device_id_type=MESH)

    def pair_sum(i):
        pair_copy(i).wait_recv()
        c2[i] = (sb[i, core].astype(F32) + r1[i].astype(F32)).astype(BF16)
        for zz in range(Z):
            @pl.when(z != zz)
            def _():
                chip_copy(i, zz).start()
        r2[i, z] = c2[i, z]

    def conv(t):
        parts = jnp.dot(g9[t], kt[...], preferred_element_type=F32)
        back = from_right(parts[:, :C]) + parts[:, C:2 * C] + from_left(parts[:, 2 * C:])
        g = gp[t, pl.ds(1, R)].reshape(M, C).astype(F32)
        dx[t] = (g + slope[t] * back).astype(BF16).reshape(R, W, C)

    def taps(low, high):
        count = high - low + 1
        g = g9[pl.ds(low, count), :, pl.ds(2 * N, N)].reshape(count * M, N)
        for i in range(3):
            if low + i < 2:
                continue
            term = jnp.dot(
                ut[:, pl.ds((low - 2 + i) * M, count * M)], g, preferred_element_type=F32)
            if high != F - 1:
                term = acc[i] + term
            if low + i > 2:
                acc[i] = term
            else:
                share_out(i, term)
                pair_copy(i).start()

    @pl.when(first)
    def _():
        cot_load.wait()

    @pl.when(first & has_below)
    def _():
        cot_low().wait_recv()

    @pl.when(first & has_above)
    def _():
        cot_high().wait_recv()

    high = F - 1
    for t in range(F - 1, -1, -1):
        @pl.when(has_next)
        def _():
            rows_copy(t).wait_recv()

        @pl.when(has_next & has_below)
        def _():
            low_copy(t).wait_recv()

        @pl.when(has_next & has_above)
        def _():
            high_copy(t).wait_recv()

        for j in range(3):
            piece = gp[t, pl.ds(2 - j, R)].reshape(M, C)
            for i in range(3):
                if t - 2 + i >= 0:
                    g9[t - 2 + i, :, pl.ds((3 * i + j) * C, C)] = piece

        if t > 0:
            conv(t)
        else:
            pl.when(has_prev)(lambda: conv(0))

        @pl.when(has_prev)
        def _():
            rows_copy(t).start()

        @pl.when(has_prev & has_above)
        def _():
            low_copy(t).start()

        @pl.when(has_prev & has_below)
        def _():
            high_copy(t).start()

        if t < 3 or high > t:
            if high == F - 1:
                pl.when(first)(activated)
            taps(t, high)
            high = t - 1
        if t < 2:
            pair_sum(1 - t)

    pair_sum(2)
    pl.when(s == 0)(lambda: conv(0))

    for i in range(3):
        for zz in range(Z):
            @pl.when(z != zz)
            def _():
                chip_arrival(i, zz).wait_recv()
        total = r2[i, 0].astype(F32)
        for zz in range(1, Z):
            total = total + r2[i, zz].astype(F32)
        dw[pl.ds(9 * i, 9)] = total

    for i in range(3):
        pair_copy(i).wait_send()
        for zz in range(Z):
            @pl.when(z != zz)
            def _():
                chip_copy(i, zz).wait_send()

    @pl.when(first & has_above)
    def _():
        cot_low().wait_send()

    @pl.when(first & has_below)
    def _():
        cot_high().wait_send()

    @pl.when(has_prev)
    def _():
        for t in range(F):
            rows_copy(t).wait_send()

    @pl.when(has_prev & has_above)
    def _():
        for t in range(F):
            low_copy(t).wait_send()

    @pl.when(has_prev & has_below)
    def _():
        for t in range(F):
            high_copy(t).wait_send()


def local(S, G, acts, kernels, cotangent):
    F, R, W, C = cotangent.shape
    share = C // G
    sp = -(-share // 16) * 16
    Z = G // 2
    M = R * W
    scale = 1.0 / math.sqrt(F * R * G * W)
    dma = pltpu.SemaphoreType.DMA
    dx, dw = pl.pallas_call(
        functools.partial(kernel, S, G, share),
        out_shape=(
            jax.ShapeDtypeStruct((F, R, W, C), BF16),
            jax.ShapeDtypeStruct((27, sp, C), F32),
        ),
        in_specs=[pl.BlockSpec(memory_space=pltpu.HBM)] * 3,
        out_specs=[pl.BlockSpec(memory_space=pltpu.VMEM)] * 2,
        scratch_shapes=[
            pltpu.VMEM((F, R, W, C), BF16),
            pltpu.VMEM((3, 3, 3, C, C), BF16),
            pltpu.VMEM((F, R + 2, W, C), BF16),
            pltpu.VMEM((F, M, 9 * C), BF16),
            pltpu.VMEM((9 * C, 3 * C), BF16),
            pltpu.VMEM((F, M, C), F32),
            pltpu.VMEM((3 * C, F * M), BF16),
            pltpu.VMEM((3, 3 * C, 3 * C), F32),
            pltpu.VMEM((3, 2, Z, 9, sp, C), BF16),
            pltpu.VMEM((3, Z, 9, sp, C), BF16),
            pltpu.VMEM((3, Z, 9, sp, C), BF16),
            pltpu.VMEM((3, Z, 9, sp, C), BF16),
            dma((F,)), dma((F,)), dma((F,)), dma((F,)), dma((F,)), dma((F,)),
            dma((2,)), dma((2,)), dma((3,)),
            dma((3,)), dma((3,)), dma((3, Z)), dma((3, Z)),
        ],
        compiler_params=pltpu.CompilerParams(
            collective_id=0, has_side_effects=True, vmem_limit_bytes=48 * 2**20
        ),
        cost_estimate=pl.CostEstimate(
            flops=4 * 27 * F * M * C * C, bytes_accessed=4 * 27 * C * C, transcendentals=F * M * C
        ),
    )(acts[0], kernels[0], cotangent)
    kernel_part = jnp.transpose(dw[:, :share], (1, 0, 2)) * scale
    return (dx[None], kernel_part[None])


def solution(mesh):
    return jax.shard_map(
        functools.partial(local, mesh.shape["section"], mesh.shape["dp"]),
        mesh=mesh,
        in_specs=(
            P("section", None, "dp", None, None),
            P("section", None, None, None, None, None),
            P(None, "dp", None, None),
        ),
        out_specs=(P("section", None, "dp", None, None), P("section", "dp", None, None)),
        check_vma=False,
    )
```

time: 50.5 us -> 45.5 us (0.901)
  Pallas kernels: 45.1 us -> 40.1 us
    pallas_call x1, Pallas kernels: 45.1 us -> 40.1 us  [local(): pl.pallas_call(functools.partial(kernel, S, G, share), out_shape=(jax.Sha...]
where the time goes in v2:
time: 45.5 us; the launch traced here: 45.3 us
  Pallas kernels  40.1 us (88%)
  local copies, waits for them, and re-layouts  3.8 us (8%)
  other arithmetic  0.71 us (2%)
  between operations  0.65 us (1%)
    pallas_call x1, Pallas kernels, local(): pl.pallas_call(functools.partial(kernel, S, G, share), out_shape=(jax.Sha...  40.1 us
    unnamed x7, local copies, waits for them, and re-layouts  3.8 us

profile of v2, /device:TPU:0, one launch (start us, length us, event | category | flops | bytes accessed | tf_op | source)
XLA Modules:
  0.0 45.3 jit_solution(5197846024897845621)
XLA Ops:
  0.6 0.0 copy-start
  0.6 1.2 %copy-done = bf16[1,3,3,3,128,128]{5,4,3,2,1,0:T(8,128)(2,1)S(1)} copy-done((bf16[1,3,3,3,128,128]{5,4,3,2,1,0:T(8,128)(2,1)S(1)}, bf16[1,3,3,3,128,128]{5,4,3,2,1,0:T(8,128)(2,1)}, u32[]{:S(2)}) %copy-start) | copy-done | bytes 884760
  1.8 0.0 copy-start.1
  1.8 1.0 %copy-done.1 = bf16[1,9,4,32,128]{4,3,2,1,0:T(8,128)(2,1)S(1)} copy-done((bf16[1,9,4,32,128]{4,3,2,1,0:T(8,128)(2,1)S(1)}, bf16[1,9,4,32,128]{4,3,2,1,0:T(8,128)(2,1)}, u32[]{:S(2)}) %copy-start.1) | copy-done | bytes 294936
  2.8 0.0 copy-start.2
  2.8 1.0 %copy-done.2 = bf16[9,4,32,128]{3,2,1,0:T(8,128)(2,1)S(1)} copy-done((bf16[9,4,32,128]{3,2,1,0:T(8,128)(2,1)S(1)}, bf16[9,4,32,128]{3,2,1,0:T(8,128)(2,1)}, u32[]{:S(2)}) %copy-start.2) | copy-done | bytes 294936
  3.7 40.1 %shard_map.50 = (bf16[9,4,32,128]{3,2,1,0:T(8,128)(2,1)S(1)}, f32[27,16,128]{2,1,0:T(8,128)S(1)}) custom-call(bf16[9,4,32,128]{3,2,1,0:T(8,128)(2,1)S(1)} %bitcast.9, bf16[3,3,3,128,128]{4,3,2,1,0:T(8,128)(2,1)S(1)} %bitcast.8, bf16[9,4,32,128]{3,2,1,0:T(8,128)(2,1)S(1)} %copy-done.2), custom_call_target="tpu_custom_call" | custom-call | flops 2038431744 | bytes 1769472 | tf_op jit(solution)/shard_map/pallas_call | solution.py:326
  43.8 0.7 %multiply_bitcast_fusion = f32[1,16,27,128]{3,1,2,0:T(8,128)} fusion(f32[27,16,128]{2,1,0:T(8,128)S(1)} %get-tuple-element.5), kind=kLoop, calls=%fused_computation | loop fusion | flops 55296 | bytes 442368 | tf_op jit(solution)/shard_map/broadcast_in_dim | solution.py:359
  44.5 0.7 %copy.6 = bf16[1,9,4,32,128]{4,3,2,1,0:T(8,128)(2,1)} copy(bf16[1,9,4,32,128]{4,3,2,1,0:T(8,128)(2,1)S(1)} %bitcast.7) | data formatting | bytes 589824
Async XLA Ops:
  0.6 1.2 %copy-start = (bf16[1,3,3,3,128,128]{5,4,3,2,1,0:T(8,128)(2,1)S(1)}, bf16[1,3,3,3,128,128]{5,4,3,2,1,0:T(8,128)(2,1)}, u32[]{:S(2)}) copy-start(bf16[1,3,3,3,128,128]{5,4,3,2,1,0:T(8,128)(2,1)} %param.4) | copy-start | bytes 2654212
  1.8 1.0 %copy-start.1 = (bf16[1,9,4,32,128]{4,3,2,1,0:T(8,128)(2,1)S(1)}, bf16[1,9,4,32,128]{4,3,2,1,0:T(8,128)(2,1)}, u32[]{:S(2)}) copy-start(bf16[1,9,4,32,128]{4,3,2,1,0:T(8,128)(2,1)} %param.3) | copy-start | bytes 884740
  2.8 1.0 %copy-start.2 = (bf16[9,4,32,128]{3,2,1,0:T(8,128)(2,1)S(1)}, bf16[9,4,32,128]{3,2,1,0:T(8,128)(2,1)}, u32[]{:S(2)}) copy-start(bf16[9,4,32,128]{3,2,1,0:T(8,128)(2,1)} %cot_h.1) | copy-start | bytes 884740

commit v3 on v2

--- a/solution.py
+++ b/solution.py
@@ -78,7 +78,9 @@
             greet(s, 2 * zz + core)
 
     acts_load.wait()
-    for t in range(F):
+
+    @pl.loop(0, F)
+    def _(t):
         x = acts[t].reshape(M, C).astype(F32)
         sig = jax.nn.sigmoid(x)
         slope[t] = sig * (1.0 + x * (1.0 - sig))
@@ -128,14 +130,15 @@
     def _():
         gp[:, pl.ds(R + 1, 1)] = jnp.zeros((F, 1, W, C), BF16)
 
-    g9[F - 1, :, pl.ds(0, 2 * N)] = jnp.zeros((M, 2 * N), BF16)
-    g9[F - 2, :, pl.ds(0, N)] = jnp.zeros((M, N), BF16)
+    g9[F + 1, :, pl.ds(0, 2 * N)] = jnp.zeros((M, 2 * N), BF16)
+    g9[F, :, pl.ds(0, N)] = jnp.zeros((M, N), BF16)
 
     kern_load.wait()
-    for i in range(3):
-        for j in range(3):
-            for k in range(3):
-                kt[pl.ds((3 * i + j) * C, C), pl.ds(k * C, C)] = kern[i, j, k].T
+
+    @pl.loop(0, 9)
+    def _(tap):
+        for k in range(3):
+            kt[pl.ds(pl.multiple_of(tap * C, C), C), pl.ds(k * C, C)] = kern[tap, k].T
 
     col = lax.rem(lax.broadcasted_iota(jnp.int32, (M, C), 0), W)
     not_first, not_last = col > 0, col < W - 1
@@ -146,14 +149,6 @@
     def from_right(v):
         return jnp.where(not_last, pltpu.roll(v, M - 1, 0), 0.0)
 
-    def activated():
-        for t in range(F):
-            x = acts[t].reshape(M, C).astype(F32)
-            u = (x * jax.nn.sigmoid(x)).astype(BF16).astype(F32)
-            for k, v in enumerate((from_left(u), u, from_right(u))):
-                ut[pl.ds(k * C, C), pl.ds(t * M, M)] = v.T.astype(BF16)
-
-    pl.when(has_next)(activated)
 
     def share_out(i, part):
         for j in range(3):
@@ -193,41 +188,24 @@
         r2[i, z] = c2[i, z]
 
     def conv(t):
-        parts = jnp.dot(g9[t], kt[...], preferred_element_type=F32)
+        parts = jnp.dot(g9[t + 2], kt[...], preferred_element_type=F32)
         back = from_right(parts[:, :C]) + parts[:, C:2 * C] + from_left(parts[:, 2 * C:])
         g = gp[t, pl.ds(1, R)].reshape(M, C).astype(F32)
         dx[t] = (g + slope[t] * back).astype(BF16).reshape(R, W, C)
 
-    def taps(low, high):
-        count = high - low + 1
-        g = g9[pl.ds(low, count), :, pl.ds(2 * N, N)].reshape(count * M, N)
-        for i in range(3):
-            if low + i < 2:
-                continue
-            term = jnp.dot(
-                ut[:, pl.ds((low - 2 + i) * M, count * M)], g, preferred_element_type=F32)
-            if high != F - 1:
-                term = acc[i] + term
-            if low + i > 2:
+    def taps(low, count, parts):
+        g = g9[pl.ds(low + 2, count), :, pl.ds(2 * N, N)].reshape(count * M, N)
+        for i in parts:
+            at = low - 2 + i
+            u = ut[at] if count == 1 else jnp.concatenate([ut[at], ut[at + 1]], axis=1)
+            term = acc[i] + jnp.dot(u, g, preferred_element_type=F32)
+            if not isinstance(low, int) or low + i > 2:
                 acc[i] = term
             else:
                 share_out(i, term)
                 pair_copy(i).start()
 
-    @pl.when(first)
-    def _():
-        cot_load.wait()
-
-    @pl.when(first & has_below)
-    def _():
-        cot_low().wait_recv()
-
-    @pl.when(first & has_above)
-    def _():
-        cot_high().wait_recv()
-
-    high = F - 1
-    for t in range(F - 1, -1, -1):
+    def frame(t):
         @pl.when(has_next)
         def _():
             rows_copy(t).wait_recv()
@@ -243,33 +221,82 @@
         for j in range(3):
             piece = gp[t, pl.ds(2 - j, R)].reshape(M, C)
             for i in range(3):
-                if t - 2 + i >= 0:
-                    g9[t - 2 + i, :, pl.ds((3 * i + j) * C, C)] = piece
-
-        if t > 0:
+                g9[t + i, :, pl.ds((3 * i + j) * C, C)] = piece
+
+        @pl.when((t > 0) | has_prev)
+        def _():
             conv(t)
+
+        @pl.when(has_prev)
+        def _():
+            rows_copy(t).start()
+
+        @pl.when(has_prev & has_above)
+        def _():
+            low_copy(t).start()
+
+        @pl.when(has_prev & has_below)
+        def _():
+            high_copy(t).start()
+
+    @pl.when(first)
+    def _():
+        cot_load.wait()
+
+    @pl.when(first & has_below)
+    def _():
+        cot_low().wait_recv()
+
+    @pl.when(first & has_above)
+    def _():
+        cot_high().wait_recv()
+
+    @pl.when(first)
+    def _():
+        @pl.loop(0, F)
+        def _(back_t):
+            frame(F - 1 - back_t)
+
+    @pl.loop(0, F)
+    def _(t):
+        x = acts[t].reshape(M, C).astype(F32)
+        u = (x * jax.nn.sigmoid(x)).astype(BF16).astype(F32)
+        for k, v in enumerate((from_left(u), u, from_right(u))):
+            ut[t, pl.ds(k * C, C)] = v.T.astype(BF16)
+
+    for i in range(3):
+        acc[i] = jnp.zeros((N, N), F32)
+
+    @pl.loop(0, F)
+    def _(back_t):
+        t = F - 1 - back_t
+
+        @pl.when(has_next)
+        def _():
+            frame(t)
+
+        if F % 2:
+            @pl.when((t > 2) & (t % 2 == 1))
+            def _():
+                taps(t, 2, range(3))
         else:
-            pl.when(has_prev)(lambda: conv(0))
-
-        @pl.when(has_prev)
-        def _():
-            rows_copy(t).start()
-
-        @pl.when(has_prev & has_above)
-        def _():
-            low_copy(t).start()
-
-        @pl.when(has_prev & has_below)
-        def _():
-            high_copy(t).start()
-
-        if t < 3 or high > t:
-            if high == F - 1:
-                pl.when(first)(activated)
-            taps(t, high)
-            high = t - 1
-        if t < 2:
-            pair_sum(1 - t)
+            @pl.when(t > 2)
+            def _():
+                taps(t, 1, range(3))
+
+        @pl.when(t == 2)
+        def _():
+            taps(2, 1, range(3))
+
+        @pl.when(t == 1)
+        def _():
+            taps(1, 1, (1, 2))
+            pair_sum(0)
+
+        @pl.when(t == 0)
+        def _():
+            taps(0, 1, (2,))
+            pair_sum(1)
 
     pair_sum(2)
     pl.when(s == 0)(lambda: conv(0))
@@ -301,17 +328,20 @@
 
     @pl.when(has_prev)
     def _():
-        for t in range(F):
+        @pl.loop(0, F)
+        def _(t):
             rows_copy(t).wait_send()
 
     @pl.when(has_prev & has_above)
     def _():
-        for t in range(F):
+        @pl.loop(0, F)
+        def _(t):
             low_copy(t).wait_send()
 
     @pl.when(has_prev & has_below)
     def _():
-        for t in range(F):
+        @pl.loop(0, F)
+        def _(t):
             high_copy(t).wait_send()
 
 
@@ -333,12 +363,12 @@
         out_specs=[pl.BlockSpec(memory_space=pltpu.VMEM)] * 2,
         scratch_shapes=[
             pltpu.VMEM((F, R, W, C), BF16),
-            pltpu.VMEM((3, 3, 3, C, C), BF16),
+            pltpu.VMEM((9, 3, C, C), BF16),
             pltpu.VMEM((F, R + 2, W, C), BF16),
-            pltpu.VMEM((F, M, 9 * C), BF16),
+            pltpu.VMEM((F + 2, M, 9 * C), BF16),
             pltpu.VMEM((9 * C, 3 * C), BF16),
             pltpu.VMEM((F, M, C), F32),
-            pltpu.VMEM((3 * C, F * M), BF16),
+            pltpu.VMEM((F, 3 * C, M), BF16),
             pltpu.VMEM((3, 3 * C, 3 * C), F32),
             pltpu.VMEM((3, 2, Z, 9, sp, C), BF16),
             pltpu.VMEM((3, Z, 9, sp, C), BF16),
@@ -349,12 +379,12 @@
             dma((3,)), dma((3,)), dma((3, Z)), dma((3, Z)),
         ],
         compiler_params=pltpu.CompilerParams(
-            collective_id=0, has_side_effects=True, vmem_limit_bytes=48 * 2**20
+            collective_id=0, has_side_effects=True, vmem_limit_bytes=64 * 2**20 - 2**18
         ),
         cost_estimate=pl.CostEstimate(
             flops=4 * 27 * F * M * C * C, bytes_accessed=4 * 27 * C * C, transcendentals=F * M * C
         ),
-    )(acts[0], kernels[0], cotangent)
+    )(acts[0], kernels[0].reshape(9, 3, C, C), cotangent)
     kernel_part = jnp.transpose(dw[:, :share], (1, 0, 2)) * scale
     return (dx[None], kernel_part[None])
 

time: 45.5 us -> 44.8 us (0.985)
  local copies, waits for them, and re-layouts: 3.8 us -> 0.72 us
  Pallas kernels: 40.1 us -> 41.6 us
  other arithmetic: 0.71 us -> 1.69 us
    unnamed x7 -> x3, local copies, waits for them, and re-layouts: 3.8 us -> 0.72 us
    pallas_call x1, Pallas kernels: 40.1 us -> 41.6 us  [local(): pl.pallas_call(functools.partial(kernel, S, G, share), out_shape=(jax.Sha...]
    broadcast_in_dim x1, other arithmetic: 0.71 us -> 1.69 us  [local(): return (dx[None], kernel_part[None])]
where the time goes in v3:
time: 44.8 us; the launch traced here: 44.6 us
  Pallas kernels  41.6 us (93%)
  other arithmetic  1.69 us (4%)
  local copies, waits for them, and re-layouts  0.72 us (2%)
  between operations  0.65 us (1%)
    pallas_call x1, Pallas kernels, local(): pl.pallas_call(functools.partial(kernel, S, G, share), out_shape=(jax.Sha...  41.6 us
    broadcast_in_dim x1, other arithmetic, local(): return (dx[None], kernel_part[None])  1.69 us

profile of v3, /device:TPU:0, one launch (start us, length us, event | category | flops | bytes accessed | tf_op | source)
XLA Modules:
  0.0 44.6 jit_solution(2811636226644516562)
XLA Ops:
  0.6 41.6 %shard_map.50 = (bf16[9,4,32,128]{3,2,1,0:T(8,128)(2,1)}, f32[27,16,128]{2,1,0:T(8,128)}) custom-call(bf16[9,4,32,128]{3,2,1,0:T(8,128)(2,1)} %bitcast.9, bf16[9,3,128,128]{3,2,1,0:T(8,128)(2,1)} %bitcast.8, bf16[9,4,32,128]{3,2,1,0:T(8,128)(2,1)} %cot_h.1), custom_call_target="tpu_custom_call" | custom-call | flops 2038431744 | bytes 1769472 | tf_op jit(solution)/shard_map/pallas_call | solution.py:356
  42.2 0.0 copy-start
  42.2 1.7 %multiply_bitcast_fusion = f32[1,16,27,128]{3,1,2,0:T(8,128)} fusion(f32[27,16,128]{2,1,0:T(8,128)} %get-tuple-element.5), kind=kLoop, calls=%fused_computation | loop fusion | flops 55296 | bytes 442368 | tf_op jit(solution)/shard_map/broadcast_in_dim | solution.py:389
  43.9 0.0 copy-done
  43.9 0.7 %copy.6 = bf16[1,9,4,32,128]{4,3,2,1,0:T(8,128)(2,1)} copy(bf16[1,9,4,32,128]{4,3,2,1,0:T(8,128)(2,1)S(1)} %bitcast.7) | data formatting | bytes 589824
Async XLA Ops:
  42.2 1.7 %copy-start = (bf16[9,4,32,128]{3,2,1,0:T(8,128)(2,1)S(1)}, bf16[9,4,32,128]{3,2,1,0:T(8,128)(2,1)}, u32[]{:S(2)}) copy-start(bf16[9,4,32,128]{3,2,1,0:T(8,128)(2,1)} %get-tuple-element.4) | copy-start | bytes 884740

commit v4 on v3

--- a/solution.py
+++ b/solution.py
@@ -140,14 +140,14 @@
         for k in range(3):
             kt[pl.ds(pl.multiple_of(tap * C, C), C), pl.ds(k * C, C)] = kern[tap, k].T
 
-    col = lax.rem(lax.broadcasted_iota(jnp.int32, (M, C), 0), W)
-    not_first, not_last = col > 0, col < W - 1
+    def column(v):
+        return lax.rem(lax.broadcasted_iota(jnp.int32, v.shape, 0), W)
 
     def from_left(v):
-        return jnp.where(not_first, pltpu.roll(v, 1, 0), 0.0)
+        return jnp.where(column(v) > 0, pltpu.roll(v, 1, 0), 0.0)
 
     def from_right(v):
-        return jnp.where(not_last, pltpu.roll(v, M - 1, 0), 0.0)
+        return jnp.where(column(v) < W - 1, pltpu.roll(v, v.shape[0] - 1, 0), 0.0)
 
 
     def share_out(i, part):
@@ -187,11 +187,13 @@
                 chip_copy(i, zz).start()
         r2[i, z] = c2[i, z]
 
-    def conv(t):
-        parts = jnp.dot(g9[t + 2], kt[...], preferred_element_type=F32)
+    def conv(t, count):
+        f, L = pl.ds(t, count), count * M
+        parts = jnp.dot(
+            g9[pl.ds(t + 2, count)].reshape(L, 9 * C), kt[...], preferred_element_type=F32)
         back = from_right(parts[:, :C]) + parts[:, C:2 * C] + from_left(parts[:, 2 * C:])
-        g = gp[t, pl.ds(1, R)].reshape(M, C).astype(F32)
-        dx[t] = (g + slope[t] * back).astype(BF16).reshape(R, W, C)
+        g = gp[f, pl.ds(1, R)].reshape(L, C).astype(F32)
+        dx[f] = (g + slope[f].reshape(L, C) * back).astype(BF16).reshape(count, R, W, C)
 
     def taps(low, count, parts):
         g = g9[pl.ds(low + 2, count), :, pl.ds(2 * N, N)].reshape(count * M, N)
@@ -205,7 +207,7 @@
                 share_out(i, term)
                 pair_copy(i).start()
 
-    def frame(t):
+    def frame(t, chain):
         @pl.when(has_next)
         def _():
             rows_copy(t).wait_recv()
@@ -223,21 +225,34 @@
             for i in range(3):
                 g9[t + i, :, pl.ds((3 * i + j) * C, C)] = piece
 
-        @pl.when((t > 0) | has_prev)
-        def _():
-            conv(t)
+        if not chain:
+            return
+        conv(t, 1)
+
+        @pl.when(has_prev & has_above)
+        def _():
+            low_copy(t).start()
+
+        @pl.when(has_prev & has_below)
+        def _():
+            high_copy(t).start()
 
         @pl.when(has_prev)
         def _():
             rows_copy(t).start()
 
-        @pl.when(has_prev & has_above)
-        def _():
-            low_copy(t).start()
-
-        @pl.when(has_prev & has_below)
-        def _():
-            high_copy(t).start()
+    def activated():
+        @pl.loop(0, F)
+        def _(t):
+            x = acts[t].reshape(M, C).astype(F32)
+            u = (x * jax.nn.sigmoid(x)).astype(BF16).astype(F32)
+            for k, v in enumerate((from_left(u), u, from_right(u))):
+                ut[t, pl.ds(k * C, C)] = v.T.astype(BF16)
+
+        for i in range(3):
+            acc[i] = jnp.zeros((N, N), F32)
+
+    pl.when(has_next)(activated)
 
     @pl.when(first)
     def _():
@@ -251,29 +266,21 @@
     def _():
         cot_high().wait_recv()
 
-    @pl.when(first)
+    @pl.when(has_prev)
     def _():
         @pl.loop(0, F)
         def _(back_t):
-            frame(F - 1 - back_t)
-
-    @pl.loop(0, F)
-    def _(t):
-        x = acts[t].reshape(M, C).astype(F32)
-        u = (x * jax.nn.sigmoid(x)).astype(BF16).astype(F32)
-        for k, v in enumerate((from_left(u), u, from_right(u))):
-            ut[t, pl.ds(k * C, C)] = v.T.astype(BF16)
-
-    for i in range(3):
-        acc[i] = jnp.zeros((N, N), F32)
+            frame(F - 1 - back_t, True)
+
+    pl.when(first)(activated)
 
     @pl.loop(0, F)
     def _(back_t):
         t = F - 1 - back_t
 
-        @pl.when(has_next)
-        def _():
-            frame(t)
+        @pl.when(s == 0)
+        def _():
+            frame(t, False)
 
         if F % 2:
             @pl.when((t > 2) & (t % 2 == 1))
@@ -299,7 +306,15 @@
             pair_sum(1)
 
     pair_sum(2)
-    pl.when(s == 0)(lambda: conv(0))
+
+    @pl.when(s == 0)
+    def _():
+        count = 3 if F % 3 == 0 else 1
+
+        @pl.loop(0, F // count)
+        def _(q):
+            conv(q * count, count)
+
 
     for i in range(3):
         for zz in range(Z):

time: 44.8 us -> 44.5 us (level)
  no operation moved by 1% of the time
where the time goes in v4:
time: 44.5 us; the launch traced here: 44.4 us
  Pallas kernels  41.3 us (93%)
  other arithmetic  1.69 us (4%)
  local copies, waits for them, and re-layouts  0.72 us (2%)
  between operations  0.65 us (1%)
    pallas_call x1, Pallas kernels, local(): pl.pallas_call(functools.partial(kernel, S, G, share), out_shape=(jax.Sha...  41.3 us
    broadcast_in_dim x1, other arithmetic, local(): return (dx[None], kernel_part[None])  1.69 us

profile of v4, /device:TPU:0, one launch (start us, length us, event | category | flops | bytes accessed | tf_op | source)
XLA Modules:
  0.0 44.4 jit_solution(539540535583021125)
XLA Ops:
  0.6 41.3 %shard_map.50 = (bf16[9,4,32,128]{3,2,1,0:T(8,128)(2,1)}, f32[27,16,128]{2,1,0:T(8,128)}) custom-call(bf16[9,4,32,128]{3,2,1,0:T(8,128)(2,1)} %bitcast.9, bf16[9,3,128,128]{3,2,1,0:T(8,128)(2,1)} %bitcast.8, bf16[9,4,32,128]{3,2,1,0:T(8,128)(2,1)} %cot_h.1), custom_call_target="tpu_custom_call" | custom-call | flops 2038431744 | bytes 1769472 | tf_op jit(solution)/shard_map/pallas_call | solution.py:371
  42.0 0.0 copy-start
  42.0 1.7 %multiply_bitcast_fusion = f32[1,16,27,128]{3,1,2,0:T(8,128)} fusion(f32[27,16,128]{2,1,0:T(8,128)} %get-tuple-element.5), kind=kLoop, calls=%fused_computation | loop fusion | flops 55296 | bytes 442368 | tf_op jit(solution)/shard_map/broadcast_in_dim | solution.py:404
  43.6 0.0 copy-done
  43.7 0.7 %copy.6 = bf16[1,9,4,32,128]{4,3,2,1,0:T(8,128)(2,1)} copy(bf16[1,9,4,32,128]{4,3,2,1,0:T(8,128)(2,1)S(1)} %bitcast.7) | data formatting | bytes 589824
Async XLA Ops:
  42.0 1.7 %copy-start = (bf16[9,4,32,128]{3,2,1,0:T(8,128)(2,1)S(1)}, bf16[9,4,32,128]{3,2,1,0:T(8,128)(2,1)}, u32[]{:S(2)}) copy-start(bf16[9,4,32,128]{3,2,1,0:T(8,128)(2,1)} %get-tuple-element.4) | copy-start | bytes 884740

commit v5 on v4

--- a/solution.py
+++ b/solution.py
@@ -207,7 +207,7 @@
                 share_out(i, term)
                 pair_copy(i).start()
 
-    def frame(t, chain):
+    def arrive(t):
         @pl.when(has_next)
         def _():
             rows_copy(t).wait_recv()
@@ -225,9 +225,7 @@
             for i in range(3):
                 g9[t + i, :, pl.ds((3 * i + j) * C, C)] = piece
 
-        if not chain:
-            return
-        conv(t, 1)
+    def send(t):
 
         @pl.when(has_prev & has_above)
         def _():
@@ -268,9 +266,19 @@
 
     @pl.when(has_prev)
     def _():
-        @pl.loop(0, F)
-        def _(back_t):
-            frame(F - 1 - back_t, True)
+        @pl.loop(0, F // 2)
+        def _(pair):
+            t = F - 2 - 2 * pair
+            arrive(t + 1)
+            arrive(t)
+            conv(t, 2)
+            send(t + 1)
+            send(t)
+
+        if F % 2:
+            arrive(0)
+            conv(0, 1)
+            send(0)
 
     pl.when(first)(activated)
 
@@ -280,7 +288,7 @@
 
         @pl.when(s == 0)
         def _():
-            frame(t, False)
+            arrive(t)
 
         if F % 2:
             @pl.when((t > 2) & (t % 2 == 1))

time: 44.5 us -> 47 us (1.056)
  Pallas kernels: 41.3 us -> 43.8 us
    pallas_call x1, Pallas kernels: 41.3 us -> 43.8 us  [local(): pl.pallas_call(functools.partial(kernel, S, G, share), out_shape=(jax.Sha...]
where the time goes in v5:
time: 47 us; the launch traced here: 46.9 us
  Pallas kernels  43.8 us (93%)
  other arithmetic  1.69 us (4%)
  local copies, waits for them, and re-layouts  0.72 us (2%)
  between operations  0.65 us (1%)
    pallas_call x1, Pallas kernels, local(): pl.pallas_call(functools.partial(kernel, S, G, share), out_shape=(jax.Sha...  43.8 us
    broadcast_in_dim x1, other arithmetic, local(): return (dx[None], kernel_part[None])  1.69 us

profile of v5, /device:TPU:0, one launch (start us, length us, event | category | flops | bytes accessed | tf_op | source)
XLA Modules:
  0.0 46.9 jit_solution(13864559907736438485)
XLA Ops:
  0.6 43.8 %shard_map.50 = (bf16[9,4,32,128]{3,2,1,0:T(8,128)(2,1)}, f32[27,16,128]{2,1,0:T(8,128)}) custom-call(bf16[9,4,32,128]{3,2,1,0:T(8,128)(2,1)} %bitcast.9, bf16[9,3,128,128]{3,2,1,0:T(8,128)(2,1)} %bitcast.8, bf16[9,4,32,128]{3,2,1,0:T(8,128)(2,1)} %cot_h.1), custom_call_target="tpu_custom_call" | custom-call | flops 2038431744 | bytes 1769472 | tf_op jit(solution)/shard_map/pallas_call | solution.py:379
  44.5 0.0 copy-start
  44.5 1.7 %multiply_bitcast_fusion = f32[1,16,27,128]{3,1,2,0:T(8,128)} fusion(f32[27,16,128]{2,1,0:T(8,128)} %get-tuple-element.5), kind=kLoop, calls=%fused_computation | loop fusion | flops 55296 | bytes 442368 | tf_op jit(solution)/shard_map/broadcast_in_dim | solution.py:412
  46.2 0.0 copy-done
  46.2 0.7 %copy.6 = bf16[1,9,4,32,128]{4,3,2,1,0:T(8,128)(2,1)} copy(bf16[1,9,4,32,128]{4,3,2,1,0:T(8,128)(2,1)S(1)} %bitcast.7) | data formatting | bytes 589824
Async XLA Ops:
  44.5 1.7 %copy-start = (bf16[9,4,32,128]{3,2,1,0:T(8,128)(2,1)S(1)}, bf16[9,4,32,128]{3,2,1,0:T(8,128)(2,1)}, u32[]{:S(2)}) copy-start(bf16[9,4,32,128]{3,2,1,0:T(8,128)(2,1)} %get-tuple-element.4) | copy-start | bytes 884740
